TPU v7x, 32 devices: a whole 2x2x4 slice. The times are simulated.
32 devices in a mesh: row: 4 (over y, core), col: 8 (over z, x).
Axes of the slice: x: 2, y: 2, z: 4, core: 2. Of those that a mesh axis runs over, the one named last changes fastest.
Arguments:
- tensor: bfloat16 [128, 384, 4096], P(None, 'col', 'row'), may hold values from -2 to 2
- first_factor: bfloat16 [64, 4096], P(None, ('row', 'col')), may hold values from -0.453125 to 0.453125
- second_factor: bfloat16 [64, 384], P(None, 'col'), may hold values from -1.4799 to 1.4799
Outputs:
- frames: float32 [64, 128], replicated
- mode_one: float32 [64, 4096], P(None, ('row', 'col'))
All inputs are finite; a program needn't handle non-finite values.
Results may differ from a plain program's by a relative error of at most 0.004.
Values may be sent and summed in bfloat16 or wider, within the bound.
No kernel may reach another device: no remote copies, remote signals or barrier semaphores. Data moves between devices by JAX's collectives and lax.ppermute only.
A program may use at most 128 MiB of HBM per device.

v0:
```python
import functools

import jax
import jax.numpy as jnp
from jax import lax
from jax.experimental import pallas as pl
from jax.experimental.pallas import tpu as pltpu
from jax.sharding import PartitionSpec as P

ridge_weight = 0.05
HIGH = lax.Precision.HIGHEST
BOTH = ("row", "col")
F32, BF16 = jnp.float32, jnp.bfloat16
VM = pltpu.VMEM
MIB = 1 << 20


def vmem():
    return pl.BlockSpec(memory_space=VM)


def anywhere():
    return pl.BlockSpec(memory_space=pl.ANY)


def smem():
    return pl.BlockSpec(memory_space=pltpu.SMEM)


def params(mib=16):
    return pltpu.CompilerParams(vmem_limit_bytes=mib * MIB)


def dot(a, b, dims, precision=None):
    return lax.dot_general(a, b, (dims, ((), ())), precision=precision, preferred_element_type=F32)


def tree_sum(values):
    while len(values) > 1:
        values = [values[n] + values[n + 1] for n in range(0, len(values), 2)]
    return values[0]


def swap(x, axes, count, offset):
    return lax.ppermute(x, axes, [(n, n ^ offset) for n in range(count)])


def swaps(x, axes, count, offsets):
    return [x] + [swap(x, axes, count, o) for o in offsets[1:]]


def offsets_of(bits):
    found = [0]
    for bit in bits:
        found = found + [f + bit for f in found]
    return found


def prepare_body(groups, t_ref, b_ref, out_ref, wide_ref, slab, sems):
    frames, cols, _ = t_ref.shape

    def fetch(n):
        return pltpu.make_async_copy(t_ref.at[pl.ds(n * 16, 16)], slab.at[n], sems.at[n])

    for n in range(groups):
        fetch(n).start()
    for j in range(cols):
        wide_ref[j] = jnp.broadcast_to(b_ref[:, j : j + 1], wide_ref.shape[1:])
    to = lax.broadcasted_iota(jnp.int32, (256, 256), 0)
    at = lax.broadcasted_iota(jnp.int32, (256, 256), 1)
    turn = jnp.where((to // 16) + (to % 16) * 16 == at, 1.0, 0.0).astype(BF16)

    def step(n, _):
        fetch(n).wait()
        for g in range(cols // 16):
            block = slab[n, :, g * 16 : g * 16 + 16, :].reshape(256, -1)
            turned = dot(turn, block, ((1,), (0,))).astype(BF16).reshape(16, 16, -1)
            out_ref[g * 16 : g * 16 + 16, pl.ds(pl.multiple_of(n * 16, 16), 16), :] = turned
        return 0

    lax.fori_loop(0, groups, step, 0)


def prepare(tensor, second):
    frames, cols, rows = tensor.shape
    components = second.shape[0]
    groups = frames // 16
    return pl.pallas_call(
        functools.partial(prepare_body, groups),
        out_shape=(VM((cols, frames, rows), BF16), VM((cols, components, 128), F32)),
        in_specs=[anywhere(), vmem()],
        out_specs=(vmem(), vmem()),
        scratch_shapes=[VM((groups, 16, cols, rows), BF16), pltpu.SemaphoreType.DMA((groups,))],
        compiler_params=params(20),
        name="prepare",
    )(tensor, second)


def place(me_ref, pieces, full_ref):
    width = pieces[0].shape[1]
    if len(pieces) == 1:
        full_ref[...] = pieces[0][...].astype(full_ref.dtype)
        return
    for d, piece in enumerate(pieces):
        at = pl.multiple_of((me_ref[0] ^ d) * width, width)
        full_ref[:, pl.ds(at, width)] = piece[...].astype(full_ref.dtype)


def assemble_body(count, me_ref, *refs):
    pieces, (full_ref, gram_ref) = refs[:count], refs[count:]
    place(me_ref, pieces, full_ref)
    full = full_ref[...]
    gram_ref[...] = dot(full, full, ((1,), (1,)))


def assemble(me, pieces, total):
    components = pieces[0].shape[0]
    return pl.pallas_call(
        functools.partial(assemble_body, len(pieces)),
        out_shape=(
            jax.ShapeDtypeStruct((components, total), BF16),
            jax.ShapeDtypeStruct((components, components), F32),
        ),
        in_specs=[smem()] + [vmem()] * len(pieces),
        out_specs=(vmem(), vmem()),
        compiler_params=params(),
        name="assemble",
    )(me, *pieces)


def project_body(span, full_ref, second_ref, t_ref, out_ref, turned_ref):
    components = full_ref.shape[0]
    cols, frames, rows = t_ref.shape
    turned_ref[...] = full_ref[...].astype(F32).T.astype(BF16)
    weights = turned_ref[...]

    def step(n, total):
        block = t_ref[pl.ds(n * span, span)].reshape(span * frames, rows)
        product = dot(block, weights, ((1,), (0,))).reshape(span, frames, components)
        scale = second_ref[pl.ds(pl.multiple_of(n * span, span), span), :]
        for s in range(span):
            total = total + product[s] * scale[s : s + 1, :]
        return total

    total = lax.fori_loop(0, cols // span, step, jnp.zeros((frames, components), F32))
    out_ref[...] = total.T


def project(full, second_turned, turned):
    cols, frames, rows = turned.shape
    components = full.shape[0]
    return pl.pallas_call(
        functools.partial(project_body, 8),
        out_shape=jax.ShapeDtypeStruct((components, frames), F32),
        in_specs=[vmem()] * 3,
        out_specs=vmem(),
        scratch_shapes=[VM((rows, components), BF16)],
        compiler_params=params(),
        name="project",
    )(full, second_turned, turned)


def inverse(matrix):
    size = matrix.shape[0]
    row_at = lax.broadcasted_iota(jnp.int32, (size, size), 0)
    col_at = lax.broadcasted_iota(jnp.int32, (size, size), 1)
    matrix = matrix + jnp.where(row_at == col_at, ridge_weight, 0.0)
    for k in range(size):
        col = matrix[:, k : k + 1]
        row = matrix[k : k + 1, :]
        pivot = 1.0 / matrix[k : k + 1, k : k + 1]
        scaled = jnp.where(col_at[:1] == k, pivot, row * pivot)
        rest = jnp.where(col_at == k, 0.0, matrix) - col * scaled
        matrix = jnp.where(row_at == k, scaled, rest)
    return matrix


def first_inverse_body(grams, seconds, me_ref, *refs):
    gram_refs, second_refs = refs[:grams], refs[grams : grams + seconds]
    out_ref, gram_ref, all_ref = refs[grams + seconds :]
    height = second_refs[0].shape[0]
    for d, piece in enumerate(second_refs):
        at = pl.multiple_of((me_ref[0] ^ d) * height, height)
        all_ref[pl.ds(at, height), :] = piece[...].astype(F32)
    every = all_ref[...].T.astype(BF16)
    gram_second = dot(every, every, ((1,), (1,)))
    gram_ref[...] = gram_second
    out_ref[...] = inverse(tree_sum([g[...] for g in gram_refs]) * gram_second)


def first_inverse(me, grams, seconds):
    size = grams[0].shape[0]
    shape = jax.ShapeDtypeStruct((size, size), F32)
    total = sum(s.shape[0] for s in seconds)
    return pl.pallas_call(
        functools.partial(first_inverse_body, len(grams), len(seconds)),
        out_shape=(shape, shape),
        in_specs=[smem()] + [vmem()] * (len(grams) + len(seconds)),
        out_specs=(vmem(), vmem()),
        scratch_shapes=[VM((total, size), F32)],
        compiler_params=params(),
        name="first_inverse",
    )(me, *grams, *seconds)


def next_inverse_body(grams, *refs):
    out_ref = refs[-1]
    out_ref[...] = inverse(tree_sum([g[...] for g in refs[:grams]]) * refs[grams][...])


def next_inverse(grams, other):
    size = other.shape[0]
    return pl.pallas_call(
        functools.partial(next_inverse_body, len(grams)),
        out_shape=jax.ShapeDtypeStruct((size, size), F32),
        in_specs=[vmem()] * (len(grams) + 1),
        out_specs=vmem(),
        compiler_params=params(),
        name="next_inverse",
    )(*grams, other)


def hand_out(me_ref, sum_ref, outs):
    width = outs[0].shape[1]
    if len(outs) == 1:
        outs[0][...] = sum_ref[...]
        return
    for d, out in enumerate(outs):
        at = pl.multiple_of((me_ref[0] ^ d) * width, width)
        out[...] = sum_ref[:, pl.ds(at, width)]


def slab_body(sums, me_ref, inverse_ref, wide_ref, t_ref, *refs):
    parts, (frames_ref, gram_ref, z_ref, *outs), sum_ref = refs[:sums], refs[sums:-1], refs[-1]
    cols, _, rows = t_ref.shape
    components = inverse_ref.shape[0]
    frames = dot(inverse_ref[...], tree_sum([p[...] for p in parts]), ((1,), (0,)), HIGH)
    frames_ref[...] = frames
    gram_ref[...] = dot(frames, frames, ((1,), (1,)), HIGH)
    high = frames.astype(BF16)
    low = (frames - high.astype(F32)).astype(BF16)
    both = jnp.concatenate([high, low], axis=0)
    span, wide = 8, 256

    def chunk(c, _):
        lanes = pl.ds(pl.multiple_of(c * wide, wide), wide)

        def step(n, total):
            for s in range(span):
                j = n * span + s
                product = dot(both, t_ref[j, :, lanes], ((1,), (0,)))
                z = product[:components] + product[components:]
                z_ref[j, :, lanes] = z
                scale = wide_ref[j]
                total = total + z * jnp.concatenate([scale, scale], axis=1)
            return total

        start = jnp.zeros((components, wide), F32)
        sum_ref[:, lanes] = lax.fori_loop(0, cols // span, step, start)
        return 0

    lax.fori_loop(0, rows // wide, chunk, 0)
    hand_out(me_ref, sum_ref, outs)


def slab(me, inverse_first, wide, turned, parts, shares):
    cols, frames, rows = turned.shape
    components = inverse_first.shape[0]
    share = jax.ShapeDtypeStruct((components, rows // shares), F32)
    return pl.pallas_call(
        functools.partial(slab_body, len(parts)),
        out_shape=(
            jax.ShapeDtypeStruct((components, frames), F32),
            jax.ShapeDtypeStruct((components, components), F32),
            VM((cols, components, rows), F32),
        )
        + (share,) * shares,
        in_specs=[smem()] + [vmem()] * (3 + len(parts)),
        out_specs=(vmem(),) * (3 + shares),
        scratch_shapes=[VM((components, rows), F32)],
        compiler_params=params(),
        name="slab",
    )(me, inverse_first, wide, turned, *parts)


def update_body(inverse_ref, *refs):
    out_ref = refs[-1]
    summed = tree_sum([p[...] for p in refs[:-1]])
    out_ref[...] = dot(inverse_ref[...], summed, ((1,), (0,)), HIGH).astype(out_ref.dtype)


def update(inverse_now, parts):
    return pl.pallas_call(
        update_body,
        out_shape=jax.ShapeDtypeStruct(parts[0].shape, BF16),
        in_specs=[vmem()] * (1 + len(parts)),
        out_specs=vmem(),
        compiler_params=params(),
        name="update",
    )(inverse_now, *parts)


def second_body(full_ref, z_ref, out_ref):
    cols, components, rows = z_ref.shape
    lane = lax.broadcasted_iota(jnp.int32, (8, 128), 1)

    def step(n, _):
        at = pl.ds(pl.multiple_of(n * 8, 8), 8)
        mine = full_ref[at, :]
        total = jnp.zeros((8, 128), F32)
        for j in range(cols):
            product = z_ref[j, at, :] * mine
            folded = tree_sum([product[:, c * 128 : c * 128 + 128] for c in range(rows // 128)])
            total = jnp.where(lane == j, jnp.sum(folded, axis=1, keepdims=True), total)
        out_ref[at, :] = total
        return 0

    lax.fori_loop(0, components // 8, step, 0)


def second(full, z):
    components = full.shape[0]
    return pl.pallas_call(
        second_body,
        out_shape=jax.ShapeDtypeStruct((components, 128), F32),
        in_specs=[vmem()] * 2,
        out_specs=vmem(),
        compiler_params=params(),
        name="second",
    )(full.astype(F32), z)


def mode_body(sums, me_ref, inverse_ref, z_ref, *refs):
    parts, outs, (sum_ref, new_ref) = refs[:sums], refs[sums:-2], refs[-2:]
    cols, components, rows = z_ref.shape
    new_ref[...] = dot(inverse_ref[...], tree_sum([p[...] for p in parts]), ((1,), (0,)), HIGH)

    def step(n, _):
        at = pl.ds(pl.multiple_of(n * 8, 8), 8)
        scale = new_ref[at, :]
        total = jnp.zeros((8, rows), F32)
        for j in range(cols):
            total = total + z_ref[j, at, :] * scale[:, j : j + 1]
        sum_ref[at, :] = total
        return 0

    lax.fori_loop(0, components // 8, step, 0)
    hand_out(me_ref, sum_ref, outs)


def mode(me, inverse_now, z, parts, shares):
    cols, components, rows = z.shape
    share = jax.ShapeDtypeStruct((components, rows // shares), F32)
    return pl.pallas_call(
        functools.partial(mode_body, len(parts)),
        out_shape=(share,) * shares,
        in_specs=[smem()] + [vmem()] * (2 + len(parts)),
        out_specs=(vmem(),) * shares,
        scratch_shapes=[VM((components, rows), F32), VM((components, 128), F32)],
        compiler_params=params(),
        name="mode",
    )(me, inverse_now, z, *parts)


def local(tensor, first_factor, second_factor):
    frame_count, col_count, row_count = tensor.shape
    row_size, col_size = lax.axis_size("row"), lax.axis_size("col")
    every = row_size * col_size
    share_rows = row_count // col_size
    direct = share_rows % 128 == 0
    shares = col_size if direct else 1
    me = lax.axis_index("col").astype(jnp.int32).reshape(1)
    row_offsets = list(range(row_size))
    col_offsets = list(range(col_size))
    col_bits = [1 << b for b in range(col_size.bit_length() - 1)]
    row_bits = [col_size << b for b in range(row_size.bit_length() - 1)]

    def gather_rows(piece):
        if direct:
            return swaps(piece, "col", col_size, col_offsets)
        return [lax.all_gather(piece, "col", axis=1, tiled=True)]

    def scatter_rows(outs):
        if direct:
            return [outs[0]] + [swap(outs[o], "col", col_size, o) for o in col_offsets[1:]]
        return [lax.psum_scatter(outs[0], "col", scatter_dimension=1, tiled=True)]

    second_turned = second_factor.T
    first_pieces = gather_rows(first_factor)
    second_pieces = swaps(second_turned, "col", col_size, col_offsets)
    turned, wide = prepare(tensor, second_factor.astype(F32))
    first_full, gram_first = assemble(me, first_pieces, row_count)
    gram_parts = swaps(gram_first, "row", row_size, row_offsets)
    frame_part = project(first_full, second_turned.astype(F32), turned)
    inverse_first, gram_second = first_inverse(me, gram_parts, second_pieces)

    stages = [col_bits[:1] + row_bits, *(col_bits[b : b + 2] for b in range(1, len(col_bits), 2))]
    parts = [frame_part]
    for bits in stages:
        parts = swaps(tree_sum(parts), BOTH, every, offsets_of(bits))
    frames, gram_frames, z, *outs = slab(me, inverse_first, wide, turned, parts, shares)

    first_parts = scatter_rows(outs)
    inverse_second = next_inverse([gram_second], gram_frames)
    new_first = update(inverse_second, first_parts)

    full, gram_new = assemble(me, gather_rows(new_first), row_count)
    new_grams = swaps(gram_new, "row", row_size, row_offsets)
    second_parts = swaps(second(full, z), "row", row_size, row_offsets)
    inverse_third = next_inverse(new_grams, gram_frames)
    final = mode(me, inverse_third, z, second_parts, shares)
    return (frames, tree_sum(scatter_rows(final)))


def solution(mesh):
    return jax.shard_map(
        local,
        mesh=mesh,
        in_specs=(P(None, "col", "row"), P(None, ("row", "col")), P(None, "col")),
        out_specs=(P(), P(None, ("row", "col"))),
        check_vma=False,
    )
```

profile of v0, /device:TPU:0, one launch (start us, length us, event | category | flops | bytes accessed | tf_op | source)
XLA Modules:
  0.0 139.7 jit_solution(16250464610931341316)
XLA Ops:
  0.6 5.1 %collective-permute-start.5 = (bf16[64,128]{1,0:T(8,128)(2,1)}, bf16[64,128]{1,0:T(8,128)(2,1)S(1)}, u32[]{:S(2)}, u32[]{:S(2)}) collective-permute-start(bf16[64,128]{1,0:T(8,128)(2,1)} %refs_0_.1), channel_id=1, source_target_pairs={{0,6},{1,7},{2,4},{3,5},{4,2},{5,3},{6,0},{7,1},{8,14},{9,15},{10,... | collective-permute-start | bytes 49160 | tf_op jit(solution)/shard_map/ppermute | solution.py:45
  6.1 3.5 %collective-permute-start.3 = (bf16[64,128]{1,0:T(8,128)(2,1)}, bf16[64,128]{1,0:T(8,128)(2,1)S(1)}, u32[]{:S(2)}, u32[]{:S(2)}) collective-permute-start(bf16[64,128]{1,0:T(8,128)(2,1)} %refs_0_.1), channel_id=1, source_target_pairs={{0,4},{1,5},{2,6},{3,7},{4,0},{5,1},{6,2},{7,3},{8,12},{9,13},{10,... | collective-permute-start | bytes 49160 | tf_op jit(solution)/shard_map/ppermute | solution.py:45
  14.7 4.6 %copy-done = bf16[128,48,1024]{2,1,0:T(8,128)(2,1)S(1)} copy-done((bf16[128,48,1024]{2,1,0:T(8,128)(2,1)S(1)}, bf16[128,48,1024]{2,1,0:T(8,128)(2,1)}, u32[]{:S(2)}) %copy-start) | copy-done | bytes 12582936
  19.2 6.1 %prepare.1 = (bf16[48,128,1024]{2,1,0:T(8,128)(2,1)S(1)}, f32[48,64,128]{2,1,0:T(8,128)S(1)}) custom-call(bf16[128,48,1024]{2,1,0:T(8,128)(2,1)S(1)} %copy-done, f32[64,48]{1,0:T(8,128)S(1)} %copy.6.b_ref), custom_call_target="tpu_custom_call" | custom-call | tf_op jit(solution)/shard_map/prepare/pallas_call | solution.py:88
  25.6 4.5 %project.1 = f32[64,128]{1,0:T(8,128)S(1)} custom-call(bf16[64,1024]{1,0:T(8,128)(2,1)S(1)} %get-tuple-element.33.full_ref, f32[48,64]{1,0:T(8,128)S(1)} %bitcast_convert_fusion.second_ref, bf16[48,128,1024]{2,1,0:T(8,128)(2,1)S(1)} %get-tuple-element.32.t_ref), custom_call_target="tpu_custom_call" | custom-call | tf_op jit(solution)/shard_map/project/pallas_call | solution.py:152
  30.3 2.6 %collective-permute-start.22 = (f32[64,128]{1,0:T(8,128)S(1)}, f32[64,128]{1,0:T(8,128)S(1)}, u32[]{:S(2)}, u32[]{:S(2)}) collective-permute-start(f32[64,128]{1,0:T(8,128)S(1)} %project.1), channel_id=1, source_target_pairs={{0,24},{1,25},{2,26},{3,27},{4,28},{5,29},{6,30},{7,31},{8,16},{9,... | collective-permute-start | bytes 98312 | tf_op jit(solution)/shard_map/ppermute | solution.py:45
  37.8 3.9 %collective-permute-start.16 = (bf16[48,64]{1,0:T(8,128)(2,1)S(1)}, bf16[48,64]{1,0:T(8,128)(2,1)S(1)}, u32[]{:S(2)}, u32[]{:S(2)}) collective-permute-start(bf16[48,64]{1,0:T(8,128)(2,1)S(1)} %bitcast.3), channel_id=1, source_target_pairs={{0,7},{1,6},{2,5},{3,4},{4,3},{5,2},{6,1},{7,0},{8,15},{9,14},{10,... | collective-permute-start | bytes 18440 | tf_op jit(solution)/shard_map/ppermute | solution.py:45
  42.0 3.9 %collective-permute-start.13 = (bf16[48,64]{1,0:T(8,128)(2,1)S(1)}, bf16[48,64]{1,0:T(8,128)(2,1)S(1)}, u32[]{:S(2)}, u32[]{:S(2)}) collective-permute-start(bf16[48,64]{1,0:T(8,128)(2,1)S(1)} %bitcast.6), channel_id=1, source_target_pairs={{0,4},{1,5},{2,6},{3,7},{4,0},{5,1},{6,2},{7,3},{8,12},{9,13},{10,... | collective-permute-start | bytes 18440 | tf_op jit(solution)/shard_map/ppermute | solution.py:45
  47.1 2.1 %collective-permute-start.26 = (f32[64,128]{1,0:T(8,128)S(1)}, f32[64,128]{1,0:T(8,128)S(1)}, u32[]{:S(2)}, u32[]{:S(2)}) collective-permute-start(f32[64,128]{1,0:T(8,128)S(1)} %add_add_fusion.1.refs_0_), channel_id=1, source_target_pairs={{0,6},{1,7},{2,4},{3,5},{4,2},{5,3},{6,0},{7,1},{8,14},{9,15},{10,... | collective-permute-start | bytes 98312 | tf_op jit(solution)/shard_map/ppermute | solution.py:45
  52.2 3.2 %collective-permute-done.11.refs_6_ = bf16[48,64]{1,0:T(8,128)(2,1)S(1)} collective-permute-done((bf16[48,64]{1,0:T(8,128)(2,1)S(1)}, bf16[48,64]{1,0:T(8,128)(2,1)S(1)}, u32[]{:S(2)}, u32[]{:S(2)}) %collective-permute-start.11) | collective-permute-done | bytes 6176 | tf_op jit(solution)/shard_map/ppermute | solution.py:45
  56.5 2.5 %collective-permute-done.10.refs_5_ = bf16[48,64]{1,0:T(8,128)(2,1)S(1)} collective-permute-done((bf16[48,64]{1,0:T(8,128)(2,1)S(1)}, bf16[48,64]{1,0:T(8,128)(2,1)S(1)}, u32[]{:S(2)}, u32[]{:S(2)}) %collective-permute-start.10) | collective-permute-done | bytes 6176 | tf_op jit(solution)/shard_map/ppermute | solution.py:45
  60.6 2.4 %collective-permute-done.8.refs_2_ = f32[64,64]{1,0:T(8,128)S(1)} collective-permute-done((f32[64,64]{1,0:T(8,128)S(1)}, f32[64,64]{1,0:T(8,128)S(1)}, u32[]{:S(2)}, u32[]{:S(2)}) %collective-permute-start.8) | collective-permute-done | bytes 16416 | tf_op jit(solution)/shard_map/ppermute | solution.py:45
  63.0 5.7 %first_inverse.1 = (f32[64,64]{1,0:T(8,128)S(1)}, f32[64,64]{1,0:T(8,128)S(1)}) custom-call(s32[1]{0:T(128)} %bitcast.me_ref, f32[64,64]{1,0:T(8,128)S(1)} %get-tuple-element.29.refs_0_, f32[64,64]{1,0:T(8,128)S(1)} %collective-permute-done.7.refs_1_, f32[64,64]{1,0:T(8,128)S(1)} %collective-permute-done.8.refs_2_, ...), custom_call_target="tpu_custom_call" | custom-call | tf_op jit(solution)/shard_map/first_inverse/pallas_call | solution.py:195
  68.7 8.0 %slab.1 = (f32[64,128]{1,0:T(8,128)}, f32[64,64]{1,0:T(8,128)S(1)}, f32[48,64,1024]{2,1,0:T(8,128)S(1)}, f32[64,128]{1,0:T(8,128)S(1)}, f32[64,128]{1,0:T(8,128)...) custom-call(s32[1]{0:T(128)} %bitcast.me_ref, ...), custom_call_target="tpu_custom_call" | custom-call | tf_op jit(solution)/shard_map/slab/pallas_call | solution.py:270
  83.7 2.7 %collective-permute-start.32 = (f32[64,128]{1,0:T(8,128)S(1)}, f32[64,128]{1,0:T(8,128)S(1)}, u32[]{:S(2)}, u32[]{:S(2)}) collective-permute-start(f32[64,128]{1,0:T(8,128)S(1)} %get-tuple-element.43), channel_id=1, source_target_pairs={{0,6},{1,7},{2,4},{3,5},{4,2},{5,3},{6,0},{7,1},{8,14},{9,15},{10,... | collective-permute-start | bytes 98312 | tf_op jit(solution)/shard_map/ppermute | solution.py:45
  87.8 5.5 %next_inverse.2.inverse_ref = f32[64,64]{1,0:T(8,128)S(1)} custom-call(f32[64,64]{1,0:T(8,128)S(1)} %get-tuple-element.35.refs_0_, f32[64,64]{1,0:T(8,128)S(1)} %get-tuple-element.36.refs_1_.refs_4_), custom_call_target="tpu_custom_call" | custom-call | tf_op jit(solution)/shard_map/next_inverse/pallas_call | solution.py:213
  93.5 3.3 %collective-permute-start.40 = (bf16[64,128]{1,0:T(8,128)(2,1)S(1)}, bf16[64,128]{1,0:T(8,128)(2,1)S(1)}, u32[]{:S(2)}, u32[]{:S(2)}) collective-permute-start(bf16[64,128]{1,0:T(8,128)(2,1)S(1)} %update.1.refs_0_), channel_id=1, source_target_pairs={{0,7},{1,6},{2,5},{3,4},{4,3},{5,2},{6,1},{7,0},{8,15},{9,14},{10,... | collective-permute-start | bytes 49160 | tf_op jit(solution)/shard_map/ppermute | solution.py:45
  98.0 3.2 %collective-permute-start.37 = (bf16[64,128]{1,0:T(8,128)(2,1)S(1)}, bf16[64,128]{1,0:T(8,128)(2,1)S(1)}, u32[]{:S(2)}, u32[]{:S(2)}) collective-permute-start(bf16[64,128]{1,0:T(8,128)(2,1)S(1)} %update.1.refs_0_), channel_id=1, source_target_pairs={{0,4},{1,5},{2,6},{3,7},{4,0},{5,1},{6,2},{7,3},{8,12},{9,13},{10,... | collective-permute-start | bytes 49160 | tf_op jit(solution)/shard_map/ppermute | solution.py:45
  113.4 3.2 %collective-permute-done.42.refs_2_ = f32[64,64]{1,0:T(8,128)S(1)} collective-permute-done((f32[64,64]{1,0:T(8,128)S(1)}, f32[64,64]{1,0:T(8,128)S(1)}, u32[]{:S(2)}, u32[]{:S(2)}) %collective-permute-start.42) | collective-permute-done | bytes 16416 | tf_op jit(solution)/shard_map/ppermute | solution.py:45
  116.6 5.5 %next_inverse.3.inverse_ref = f32[64,64]{1,0:T(8,128)S(1)} custom-call(f32[64,64]{1,0:T(8,128)S(1)} %get-tuple-element.45.refs_0_, f32[64,64]{1,0:T(8,128)S(1)} %collective-permute-done.41.refs_1_, f32[64,64]{1,0:T(8,128)S(1)} %collective-permute-done.42.refs_2_, f32[64,64]{1,0:T(8,128)S(1)} %collective-permute-done.43.refs_3_, ...), custom_call_target="tpu_custom_call" | custom-call | tf_op jit(solution)/shard_map/next_inverse/pallas_call | solution.py:213
  124.7 2.6 %collective-permute-start.49 = (f32[64,128]{1,0:T(8,128)S(1)}, f32[64,128]{1,0:T(8,128)S(1)}, u32[]{:S(2)}, u32[]{:S(2)}) collective-permute-start(f32[64,128]{1,0:T(8,128)S(1)} %get-tuple-element.51), channel_id=1, source_target_pairs={{0,3},{1,2},{2,1},{3,0},{4,7},{5,6},{6,5},{7,4},{8,11},{9,10},{10,... | collective-permute-start | bytes 98312 | tf_op jit(solution)/shard_map/ppermute | solution.py:45
  127.7 2.8 %collective-permute-start.51 = (f32[64,128]{1,0:T(8,128)S(1)}, f32[64,128]{1,0:T(8,128)S(1)}, u32[]{:S(2)}, u32[]{:S(2)}) collective-permute-start(f32[64,128]{1,0:T(8,128)S(1)} %get-tuple-element.53), channel_id=1, source_target_pairs={{0,5},{1,4},{2,7},{3,6},{4,1},{5,0},{6,3},{7,2},{8,13},{9,12},{10,... | collective-permute-start | bytes 98312 | tf_op jit(solution)/shard_map/ppermute | solution.py:45
  132.5 2.4 %collective-permute-start.53 = (f32[64,128]{1,0:T(8,128)S(1)}, f32[64,128]{1,0:T(8,128)S(1)}, u32[]{:S(2)}, u32[]{:S(2)}) collective-permute-start(f32[64,128]{1,0:T(8,128)S(1)} %get-tuple-element.55), channel_id=1, source_target_pairs={{0,7},{1,6},{2,5},{3,4},{4,3},{5,2},{6,1},{7,0},{8,15},{9,14},{10,... | collective-permute-start | bytes 98312 | tf_op jit(solution)/shard_map/ppermute | solution.py:45
  136.2 2.9 %collective-permute-done.53 = f32[64,128]{1,0:T(8,128)S(1)} collective-permute-done((f32[64,128]{1,0:T(8,128)S(1)}, f32[64,128]{1,0:T(8,128)S(1)}, u32[]{:S(2)}, u32[]{:S(2)}) %collective-permute-start.53) | collective-permute-done | bytes 32800 | tf_op jit(solution)/shard_map/ppermute | solution.py:45
  (106 shorter events, 46.9 us)
Async XLA Ops:
  0.6 11.0 %collective-permute-start.5 = (bf16[64,128]{1,0:T(8,128)(2,1)}, bf16[64,128]{1,0:T(8,128)(2,1)S(1)}, u32[]{:S(2)}, u32[]{:S(2)}) collective-permute-start(bf16[64,128]{1,0:T(8,128)(2,1)} %refs_0_.1), channel_id=1, source_target_pairs={{0,6},{1,7},{2,4},{3,5},{4,2},{5,3},{6,0},{7,1},{8,14},{9,15},{10,... | collective-permute-start | bytes 49160 | tf_op jit(solution)/shard_map/ppermute | solution.py:45
  6.1 19.2 %collective-permute-start.3 = (bf16[64,128]{1,0:T(8,128)(2,1)}, bf16[64,128]{1,0:T(8,128)(2,1)S(1)}, u32[]{:S(2)}, u32[]{:S(2)}) collective-permute-start(bf16[64,128]{1,0:T(8,128)(2,1)} %refs_0_.1), channel_id=1, source_target_pairs={{0,4},{1,5},{2,6},{3,7},{4,0},{5,1},{6,2},{7,3},{8,12},{9,13},{10,... | collective-permute-start | bytes 49160 | tf_op jit(solution)/shard_map/ppermute | solution.py:45
  9.6 15.7 %collective-permute-start.2 = (bf16[64,128]{1,0:T(8,128)(2,1)}, bf16[64,128]{1,0:T(8,128)(2,1)S(1)}, u32[]{:S(2)}, u32[]{:S(2)}) collective-permute-start(bf16[64,128]{1,0:T(8,128)(2,1)} %refs_0_.1), channel_id=1, source_target_pairs={{0,3},{1,2},{2,1},{3,0},{4,7},{5,6},{6,5},{7,4},{8,11},{9,10},{10,... | collective-permute-start | bytes 49160 | tf_op jit(solution)/shard_map/ppermute | solution.py:45
  9.6 15.8 %collective-permute-start.1 = (bf16[64,128]{1,0:T(8,128)(2,1)}, bf16[64,128]{1,0:T(8,128)(2,1)S(1)}, u32[]{:S(2)}, u32[]{:S(2)}) collective-permute-start(bf16[64,128]{1,0:T(8,128)(2,1)} %refs_0_.1), channel_id=1, source_target_pairs={{0,2},{1,3},{2,0},{3,1},{4,6},{5,7},{6,4},{7,5},{8,10},{9,11},{10,... | collective-permute-start | bytes 49160 | tf_op jit(solution)/shard_map/ppermute | solution.py:45
  11.6 13.8 %collective-permute-start = (bf16[64,128]{1,0:T(8,128)(2,1)}, bf16[64,128]{1,0:T(8,128)(2,1)S(1)}, u32[]{:S(2)}, u32[]{:S(2)}) collective-permute-start(bf16[64,128]{1,0:T(8,128)(2,1)} %refs_0_.1), channel_id=1, source_target_pairs={{0,1},{1,0},{2,3},{3,2},{4,5},{5,4},{6,7},{7,6},{8,9},{9,8},{10,11... | collective-permute-start | bytes 49160 | tf_op jit(solution)/shard_map/ppermute | solution.py:45
  13.1 12.3 %collective-permute-start.6 = (bf16[64,128]{1,0:T(8,128)(2,1)}, bf16[64,128]{1,0:T(8,128)(2,1)S(1)}, u32[]{:S(2)}, u32[]{:S(2)}) collective-permute-start(bf16[64,128]{1,0:T(8,128)(2,1)} %refs_0_.1), channel_id=1, source_target_pairs={{0,7},{1,6},{2,5},{3,4},{4,3},{5,2},{6,1},{7,0},{8,15},{9,14},{10,... | collective-permute-start | bytes 49160 | tf_op jit(solution)/shard_map/ppermute | solution.py:45
  36.6 9.3 %collective-permute-start.17 = (f32[64,128]{1,0:T(8,128)S(1)}, f32[64,128]{1,0:T(8,128)S(1)}, u32[]{:S(2)}, u32[]{:S(2)}) collective-permute-start(f32[64,128]{1,0:T(8,128)S(1)} %project.1), channel_id=1, source_target_pairs={{0,1},{1,0},{2,3},{3,2},{4,5},{5,4},{6,7},{7,6},{8,9},{9,8},{10,11... | collective-permute-start | bytes 98312 | tf_op jit(solution)/shard_map/ppermute | solution.py:45
  37.8 9.3 %collective-permute-start.16 = (bf16[48,64]{1,0:T(8,128)(2,1)S(1)}, bf16[48,64]{1,0:T(8,128)(2,1)S(1)}, u32[]{:S(2)}, u32[]{:S(2)}) collective-permute-start(bf16[48,64]{1,0:T(8,128)(2,1)S(1)} %bitcast.3), channel_id=1, source_target_pairs={{0,7},{1,6},{2,5},{3,4},{4,3},{5,2},{6,1},{7,0},{8,15},{9,14},{10,... | collective-permute-start | bytes 18440 | tf_op jit(solution)/shard_map/ppermute | solution.py:45
  42.0 8.2 %collective-permute-start.13 = (bf16[48,64]{1,0:T(8,128)(2,1)S(1)}, bf16[48,64]{1,0:T(8,128)(2,1)S(1)}, u32[]{:S(2)}, u32[]{:S(2)}) collective-permute-start(bf16[48,64]{1,0:T(8,128)(2,1)S(1)} %bitcast.6), channel_id=1, source_target_pairs={{0,4},{1,5},{2,6},{3,7},{4,0},{5,1},{6,2},{7,3},{8,12},{9,13},{10,... | collective-permute-start | bytes 18440 | tf_op jit(solution)/shard_map/ppermute | solution.py:45
  47.0 13.5 %collective-permute-start.9 = (f32[64,64]{1,0:T(8,128)S(1)}, f32[64,64]{1,0:T(8,128)S(1)}, u32[]{:S(2)}, u32[]{:S(2)}) collective-permute-start(f32[64,64]{1,0:T(8,128)S(1)} %get-tuple-element.29.refs_0_), channel_id=1, source_target_pairs={{0,24},{8,16},{16,8},{24,0},{1,25},{9,17},{17,9},{25,1},{2,26},{10... | collective-permute-start | bytes 49160 | tf_op jit(solution)/shard_map/ppermute | solution.py:45
  47.1 21.5 %collective-permute-start.26 = (f32[64,128]{1,0:T(8,128)S(1)}, f32[64,128]{1,0:T(8,128)S(1)}, u32[]{:S(2)}, u32[]{:S(2)}) collective-permute-start(f32[64,128]{1,0:T(8,128)S(1)} %add_add_fusion.1.refs_0_), channel_id=1, source_target_pairs={{0,6},{1,7},{2,4},{3,5},{4,2},{5,3},{6,0},{7,1},{8,14},{9,15},{10,... | collective-permute-start | bytes 98312 | tf_op jit(solution)/shard_map/ppermute | solution.py:45
  49.2 19.4 %collective-permute-start.25 = (f32[64,128]{1,0:T(8,128)S(1)}, f32[64,128]{1,0:T(8,128)S(1)}, u32[]{:S(2)}, u32[]{:S(2)}) collective-permute-start(f32[64,128]{1,0:T(8,128)S(1)} %add_add_fusion.1.refs_0_), channel_id=1, source_target_pairs={{0,4},{1,5},{2,6},{3,7},{4,0},{5,1},{6,2},{7,3},{8,12},{9,13},{10,... | collective-permute-start | bytes 98312 | tf_op jit(solution)/shard_map/ppermute | solution.py:45
  50.1 18.5 %collective-permute-start.24 = (f32[64,128]{1,0:T(8,128)S(1)}, f32[64,128]{1,0:T(8,128)S(1)}, u32[]{:S(2)}, u32[]{:S(2)}) collective-permute-start(f32[64,128]{1,0:T(8,128)S(1)} %add_add_fusion.1.refs_0_), channel_id=1, source_target_pairs={{0,2},{1,3},{2,0},{3,1},{4,6},{5,7},{6,4},{7,5},{8,10},{9,11},{10,... | collective-permute-start | bytes 98312 | tf_op jit(solution)/shard_map/ppermute | solution.py:45
  77.8 8.5 %collective-permute-start.28 = (f32[64,128]{1,0:T(8,128)S(1)}, f32[64,128]{1,0:T(8,128)S(1)}, u32[]{:S(2)}, u32[]{:S(2)}) collective-permute-start(f32[64,128]{1,0:T(8,128)S(1)} %get-tuple-element.39), channel_id=1, source_target_pairs={{0,2},{1,3},{2,0},{3,1},{4,6},{5,7},{6,4},{7,5},{8,10},{9,11},{10,... | collective-permute-start | bytes 98312 | tf_op jit(solution)/shard_map/ppermute | solution.py:45
  78.7 14.6 %collective-permute-start.29 = (f32[64,128]{1,0:T(8,128)S(1)}, f32[64,128]{1,0:T(8,128)S(1)}, u32[]{:S(2)}, u32[]{:S(2)}) collective-permute-start(f32[64,128]{1,0:T(8,128)S(1)} %get-tuple-element.40), channel_id=1, source_target_pairs={{0,3},{1,2},{2,1},{3,0},{4,7},{5,6},{6,5},{7,4},{8,11},{9,10},{10,... | collective-permute-start | bytes 98312 | tf_op jit(solution)/shard_map/ppermute | solution.py:45
  80.2 13.1 %collective-permute-start.30 = (f32[64,128]{1,0:T(8,128)S(1)}, f32[64,128]{1,0:T(8,128)S(1)}, u32[]{:S(2)}, u32[]{:S(2)}) collective-permute-start(f32[64,128]{1,0:T(8,128)S(1)} %get-tuple-element.41), channel_id=1, source_target_pairs={{0,4},{1,5},{2,6},{3,7},{4,0},{5,1},{6,2},{7,3},{8,12},{9,13},{10,... | collective-permute-start | bytes 98312 | tf_op jit(solution)/shard_map/ppermute | solution.py:45
  82.0 11.3 %collective-permute-start.31 = (f32[64,128]{1,0:T(8,128)S(1)}, f32[64,128]{1,0:T(8,128)S(1)}, u32[]{:S(2)}, u32[]{:S(2)}) collective-permute-start(f32[64,128]{1,0:T(8,128)S(1)} %get-tuple-element.42), channel_id=1, source_target_pairs={{0,5},{1,4},{2,7},{3,6},{4,1},{5,0},{6,3},{7,2},{8,13},{9,12},{10,... | collective-permute-start | bytes 98312 | tf_op jit(solution)/shard_map/ppermute | solution.py:45
  83.7 9.6 %collective-permute-start.32 = (f32[64,128]{1,0:T(8,128)S(1)}, f32[64,128]{1,0:T(8,128)S(1)}, u32[]{:S(2)}, u32[]{:S(2)}) collective-permute-start(f32[64,128]{1,0:T(8,128)S(1)} %get-tuple-element.43), channel_id=1, source_target_pairs={{0,6},{1,7},{2,4},{3,5},{4,2},{5,3},{6,0},{7,1},{8,14},{9,15},{10,... | collective-permute-start | bytes 98312 | tf_op jit(solution)/shard_map/ppermute | solution.py:45
  93.5 8.6 %collective-permute-start.40 = (bf16[64,128]{1,0:T(8,128)(2,1)S(1)}, bf16[64,128]{1,0:T(8,128)(2,1)S(1)}, u32[]{:S(2)}, u32[]{:S(2)}) collective-permute-start(bf16[64,128]{1,0:T(8,128)(2,1)S(1)} %update.1.refs_0_), channel_id=1, source_target_pairs={{0,7},{1,6},{2,5},{3,4},{4,3},{5,2},{6,1},{7,0},{8,15},{9,14},{10,... | collective-permute-start | bytes 49160 | tf_op jit(solution)/shard_map/ppermute | solution.py:45
  109.4 12.7 %collective-permute-start.46 = (f32[64,128]{1,0:T(8,128)S(1)}, f32[64,128]{1,0:T(8,128)S(1)}, u32[]{:S(2)}, u32[]{:S(2)}) collective-permute-start(f32[64,128]{1,0:T(8,128)S(1)} %second.1.refs_0_), channel_id=1, source_target_pairs={{0,24},{8,16},{16,8},{24,0},{1,25},{9,17},{17,9},{25,1},{2,26},{10... | collective-permute-start | bytes 98312 | tf_op jit(solution)/shard_map/ppermute | solution.py:45
  111.1 10.9 %collective-permute-start.45 = (f32[64,128]{1,0:T(8,128)S(1)}, f32[64,128]{1,0:T(8,128)S(1)}, u32[]{:S(2)}, u32[]{:S(2)}) collective-permute-start(f32[64,128]{1,0:T(8,128)S(1)} %second.1.refs_0_), channel_id=1, source_target_pairs={{0,16},{8,24},{16,0},{24,8},{1,17},{9,25},{17,1},{25,9},{2,18},{10... | collective-permute-start | bytes 98312 | tf_op jit(solution)/shard_map/ppermute | solution.py:45
  112.7 9.4 %collective-permute-start.44 = (f32[64,128]{1,0:T(8,128)S(1)}, f32[64,128]{1,0:T(8,128)S(1)}, u32[]{:S(2)}, u32[]{:S(2)}) collective-permute-start(f32[64,128]{1,0:T(8,128)S(1)} %second.1.refs_0_), channel_id=1, source_target_pairs={{0,8},{8,0},{16,24},{24,16},{1,9},{9,1},{17,25},{25,17},{2,10},{10... | collective-permute-start | bytes 98312 | tf_op jit(solution)/shard_map/ppermute | solution.py:45
  124.6 7.9 %collective-permute-start.48 = (f32[64,128]{1,0:T(8,128)S(1)}, f32[64,128]{1,0:T(8,128)S(1)}, u32[]{:S(2)}, u32[]{:S(2)}) collective-permute-start(f32[64,128]{1,0:T(8,128)S(1)} %get-tuple-element.50), channel_id=1, source_target_pairs={{0,2},{1,3},{2,0},{3,1},{4,6},{5,7},{6,4},{7,5},{8,10},{9,11},{10,... | collective-permute-start | bytes 98312 | tf_op jit(solution)/shard_map/ppermute | solution.py:45
  124.7 10.2 %collective-permute-start.49 = (f32[64,128]{1,0:T(8,128)S(1)}, f32[64,128]{1,0:T(8,128)S(1)}, u32[]{:S(2)}, u32[]{:S(2)}) collective-permute-start(f32[64,128]{1,0:T(8,128)S(1)} %get-tuple-element.51), channel_id=1, source_target_pairs={{0,3},{1,2},{2,1},{3,0},{4,7},{5,6},{6,5},{7,4},{8,11},{9,10},{10,... | collective-permute-start | bytes 98312 | tf_op jit(solution)/shard_map/ppermute | solution.py:45
  (33 other events, 218.0 us)
where the time goes:
time: 140 us
  starting transfers between devices  74 us (53%)
  Pallas kernels  38.8 us (28%)
  waiting for transfers between devices  19.3 us (14%)
  local copies, waits for them, and re-layouts  5.37 us (4%)
    ppermute x54, starting transfers between devices, swap(): return lax.ppermute(x, axes, [(n, n ^ offset) for n in range(count)])  74 us
    ppermute x54, waiting for transfers between devices, swap(): return lax.ppermute(x, axes, [(n, n ^ offset) for n in range(count)])  19.3 us
    pallas_call x2, Pallas kernels, next_inverse(): pl.pallas_call(functools.partial(next_inverse_body, len(grams)), out_shap...  10.9 us
    pallas_call x1, Pallas kernels, slab(): pl.pallas_call(functools.partial(slab_body, len(parts)), out_shape=(jax.S...  7.99 us
    pallas_call x1, Pallas kernels, prepare(): pl.pallas_call(functools.partial(prepare_body, groups), out_shape=(VM((co...  6.1 us
    pallas_call x1, Pallas kernels, first_inverse(): pl.pallas_call(functools.partial(first_inverse_body, len(grams), len(seco...  5.67 us
    unnamed x6, local copies, waits for them, and re-layouts  4.59 us
    pallas_call x1, Pallas kernels, project(): pl.pallas_call(functools.partial(project_body, 8), out_shape=jax.ShapeDty...  4.48 us
  transfers between devices with their start and end apart: 54, of which 9 were waited for; matrix products, arithmetic and copies ran while one was open for 1% of the time, Pallas kernels for 17%

commit v1 on v0

v1 whole, which is shorter than its diff:
```python
import functools

import jax
import jax.numpy as jnp
from jax import lax
from jax.experimental import pallas as pl
from jax.experimental.pallas import tpu as pltpu
from jax.sharding import PartitionSpec as P

ridge_weight = 0.05
HIGH = lax.Precision.HIGHEST
BOTH = ("row", "col")
F32, BF16 = jnp.float32, jnp.bfloat16
VM = pltpu.VMEM
MIB = 1 << 20


def vmem():
    return pl.BlockSpec(memory_space=VM)


def hbm():
    return pl.BlockSpec(memory_space=pltpu.HBM)


def params(mib=16):
    return pltpu.CompilerParams(vmem_limit_bytes=mib * MIB)


def dot(a, b, dims, precision=None):
    return lax.dot_general(a, b, (dims, ((), ())), precision=precision, preferred_element_type=F32)


def tree_sum(values):
    while len(values) > 1:
        values = [values[n] + values[n + 1] for n in range(0, len(values), 2)]
    return values[0]


def exchange(x, axes):
    return lax.all_to_all(x, axes, 0, 0)


def prepare_body(groups, t_ref, b_ref, out_ref, wide_ref, slab, sems):
    frames, cols, _ = t_ref.shape

    def fetch(n):
        return pltpu.make_async_copy(t_ref.at[pl.ds(n * 16, 16)], slab.at[n], sems.at[n])

    for n in range(groups):
        fetch(n).start()
    for j in range(cols):
        wide_ref[j] = jnp.broadcast_to(b_ref[:, j : j + 1], wide_ref.shape[1:])
    to = lax.broadcasted_iota(jnp.int32, (256, 256), 0)
    at = lax.broadcasted_iota(jnp.int32, (256, 256), 1)
    turn = jnp.where((to // 16) + (to % 16) * 16 == at, 1.0, 0.0).astype(BF16)

    def step(n, _):
        fetch(n).wait()
        for g in range(cols // 16):
            block = slab[n, :, g * 16 : g * 16 + 16, :].reshape(256, -1)
            turned = dot(turn, block, ((1,), (0,))).astype(BF16).reshape(16, 16, -1)
            out_ref[g * 16 : g * 16 + 16, pl.ds(pl.multiple_of(n * 16, 16), 16), :] = turned
        return 0

    lax.fori_loop(0, groups, step, 0)


def prepare(tensor, second):
    frames, cols, rows = tensor.shape
    components = second.shape[0]
    groups = frames // 16
    return pl.pallas_call(
        functools.partial(prepare_body, groups),
        out_shape=(VM((cols, frames, rows), BF16), VM((cols, components, 128), F32)),
        in_specs=[hbm(), vmem()],
        out_specs=(vmem(), vmem()),
        scratch_shapes=[VM((groups, 16, cols, rows), BF16), pltpu.SemaphoreType.DMA((groups,))],
        compiler_params=params(20),
        name="prepare",
    )(tensor, second)


def copies(ref, value):
    for n in range(ref.shape[0]):
        ref[n] = value


def assemble_body(pieces_ref, others_ref, full_ref, gram_ref, other_ref):
    count, components, width = pieces_ref.shape
    for n in range(count):
        full_ref[:, n * width : n * width + width] = pieces_ref[n]
    full = full_ref[...]
    gram = dot(full, full, ((1,), (1,)))
    copies(gram_ref, jnp.concatenate([gram, gram], axis=1))
    total = jnp.zeros(other_ref.shape, F32)
    for n in range(others_ref.shape[0]):
        other = others_ref[n]
        total = total + dot(other, other, ((1,), (1,)))
    other_ref[...] = total


def assemble(pieces, others, spread):
    count, components, width = pieces.shape
    square = (components, components)
    return pl.pallas_call(
        assemble_body,
        out_shape=(
            jax.ShapeDtypeStruct((components, count * width), BF16),
            jax.ShapeDtypeStruct((spread, components, 2 * components), F32),
            jax.ShapeDtypeStruct(square, F32),
        ),
        in_specs=[vmem(), vmem()],
        out_specs=(vmem(),) * 3,
        compiler_params=params(),
        name="assemble",
    )(pieces, others)


def project_body(span, full_ref, second_ref, t_ref, out_ref, turned_ref):
    components = full_ref.shape[0]
    cols, frames, rows = t_ref.shape
    turned_ref[...] = full_ref[...].astype(F32).T.astype(BF16)
    weights = turned_ref[...]

    def step(n, total):
        block = t_ref[pl.ds(n * span, span)].reshape(span * frames, rows)
        product = dot(block, weights, ((1,), (0,))).reshape(span, frames, components)
        scale = second_ref[pl.ds(pl.multiple_of(n * span, span), span), :]
        for s in range(span):
            total = total + product[s] * scale[s : s + 1, :]
        return total

    total = lax.fori_loop(0, cols // span, step, jnp.zeros((frames, components), F32))
    out_ref[...] = total.T


def project(full, second_turned, turned):
    cols, frames, rows = turned.shape
    components = full.shape[0]
    return pl.pallas_call(
        functools.partial(project_body, 8),
        out_shape=jax.ShapeDtypeStruct((components, frames), F32),
        in_specs=[vmem()] * 3,
        out_specs=vmem(),
        scratch_shapes=[VM((rows, components), BF16)],
        compiler_params=params(),
        name="project",
    )(full, second_turned, turned)


def inverse(matrix):
    size = matrix.shape[0]
    row_at = lax.broadcasted_iota(jnp.int32, (size, size), 0)
    col_at = lax.broadcasted_iota(jnp.int32, (size, size), 1)
    matrix = matrix + jnp.where(row_at == col_at, ridge_weight, 0.0)
    for k in range(size):
        col = matrix[:, k : k + 1]
        row = matrix[k : k + 1, :]
        pivot = 1.0 / matrix[k : k + 1, k : k + 1]
        scaled = jnp.where(col_at[:1] == k, pivot, row * pivot)
        rest = jnp.where(col_at == k, 0.0, matrix) - col * scaled
        matrix = jnp.where(row_at == k, scaled, rest)
    return matrix


def inverse_body(grams_ref, other_ref, out_ref):
    gram = tree_sum([grams_ref[n] for n in range(grams_ref.shape[0])])
    out_ref[...] = inverse(gram[:, : other_ref.shape[0]] * other_ref[...])


def inverse_of(grams, other):
    return pl.pallas_call(
        inverse_body,
        out_shape=jax.ShapeDtypeStruct(other.shape, F32),
        in_specs=[vmem(), vmem()],
        out_specs=vmem(),
        compiler_params=params(),
        name="inverse",
    )(grams, other)


def spread_body(parts_ref, out_ref):
    copies(out_ref, tree_sum([parts_ref[n] for n in range(parts_ref.shape[0])]))


def spread_sum(parts):
    return pl.pallas_call(
        spread_body,
        out_shape=jax.ShapeDtypeStruct(parts.shape, F32),
        in_specs=[vmem()],
        out_specs=vmem(),
        compiler_params=params(),
        name="spread_sum",
    )(parts)


def hand_out(sum_ref, out_ref):
    count, _, width = out_ref.shape
    for n in range(count):
        out_ref[n] = sum_ref[:, n * width : n * width + width]


def slab_body(inverse_ref, sum_in_ref, wide_ref, t_ref, frames_ref, gram_ref, z_ref, out_ref, sum_ref):
    cols, _, rows = t_ref.shape
    components = inverse_ref.shape[0]
    frames = dot(inverse_ref[...], sum_in_ref[...], ((1,), (0,)), HIGH)
    frames_ref[...] = frames
    gram_ref[...] = dot(frames, frames, ((1,), (1,)), HIGH)
    high = frames.astype(BF16)
    low = (frames - high.astype(F32)).astype(BF16)
    both = jnp.concatenate([high, low], axis=0)
    span, wide = 8, 256

    def chunk(c, _):
        lanes = pl.ds(pl.multiple_of(c * wide, wide), wide)

        def step(n, total):
            for s in range(span):
                j = n * span + s
                product = dot(both, t_ref[j, :, lanes], ((1,), (0,)))
                z = product[:components] + product[components:]
                z_ref[j, :, lanes] = z
                scale = wide_ref[j]
                total = total + z * jnp.concatenate([scale, scale], axis=1)
            return total

        start = jnp.zeros((components, wide), F32)
        sum_ref[:, lanes] = lax.fori_loop(0, cols // span, step, start)
        return 0

    lax.fori_loop(0, rows // wide, chunk, 0)
    hand_out(sum_ref, out_ref)


def slab(inverse_first, frame_sum, wide, turned, shares):
    cols, frames, rows = turned.shape
    components = inverse_first.shape[0]
    return pl.pallas_call(
        slab_body,
        out_shape=(
            jax.ShapeDtypeStruct((components, frames), F32),
            jax.ShapeDtypeStruct((components, components), F32),
            VM((cols, components, rows), F32),
            jax.ShapeDtypeStruct((shares, components, rows // shares), F32),
        ),
        in_specs=[vmem()] * 4,
        out_specs=(vmem(),) * 4,
        scratch_shapes=[VM((components, rows), F32)],
        compiler_params=params(),
        name="slab",
    )(inverse_first, frame_sum, wide, turned)


def update_body(inverse_ref, parts_ref, out_ref):
    summed = tree_sum([parts_ref[n] for n in range(parts_ref.shape[0])])
    new = dot(inverse_ref[...], summed, ((1,), (0,)), HIGH).astype(BF16)
    copies(out_ref, new)


def update(inverse_now, parts, spread):
    return pl.pallas_call(
        update_body,
        out_shape=jax.ShapeDtypeStruct((spread,) + parts.shape[1:], BF16),
        in_specs=[vmem()] * 2,
        out_specs=vmem(),
        compiler_params=params(),
        name="update",
    )(inverse_now, parts)


def second_body(pieces_ref, z_ref, out_ref, full_ref):
    cols, components, rows = z_ref.shape
    count, _, width = pieces_ref.shape
    gram = jnp.zeros((components, components), F32)
    for n in range(count):
        piece = pieces_ref[n]
        gram = gram + dot(piece, piece, ((1,), (1,)))
        full_ref[:, n * width : n * width + width] = piece.astype(F32)
    lane = lax.broadcasted_iota(jnp.int32, (8, 128), 1)

    def step(n, _):
        at = pl.ds(pl.multiple_of(n * 8, 8), 8)
        mine = full_ref[at, :]
        total = jnp.zeros((8, 128), F32)
        for j in range(cols):
            product = z_ref[j, at, :] * mine
            folded = tree_sum([product[:, c * 128 : c * 128 + 128] for c in range(rows // 128)])
            total = jnp.where(lane == j, jnp.sum(folded, axis=1, keepdims=True), total)
        out_ref[0, at, :] = total
        return 0

    lax.fori_loop(0, components // 8, step, 0)
    both = jnp.concatenate([out_ref[0][:, :components], gram], axis=1)
    copies(out_ref, both)


def second(pieces, z, spread):
    cols, components, rows = z.shape
    return pl.pallas_call(
        second_body,
        out_shape=jax.ShapeDtypeStruct((spread, components, 2 * components), F32),
        in_specs=[vmem()] * 2,
        out_specs=vmem(),
        scratch_shapes=[VM((components, rows), F32)],
        compiler_params=params(),
        name="second",
    )(pieces, z)


def mode_body(parts_ref, gram_frames_ref, z_ref, out_ref, sum_ref, new_ref):
    cols, components, rows = z_ref.shape
    summed = tree_sum([parts_ref[n] for n in range(parts_ref.shape[0])])
    solver = inverse(summed[:, components:] * gram_frames_ref[...])
    new_ref[...] = dot(solver, summed, ((1,), (0,)), HIGH)

    def step(n, _):
        at = pl.ds(pl.multiple_of(n * 8, 8), 8)
        scale = new_ref[at, :]
        total = jnp.zeros((8, rows), F32)
        for j in range(cols):
            total = total + z_ref[j, at, :] * scale[:, j : j + 1]
        sum_ref[at, :] = total
        return 0

    lax.fori_loop(0, components // 8, step, 0)
    hand_out(sum_ref, out_ref)


def mode(parts, gram_frames, z, shares):
    cols, components, rows = z.shape
    return pl.pallas_call(
        mode_body,
        out_shape=jax.ShapeDtypeStruct((shares, components, rows // shares), F32),
        in_specs=[vmem()] * 3,
        out_specs=vmem(),
        scratch_shapes=[VM((components, rows), F32), VM((components, 2 * components), F32)],
        compiler_params=params(),
        name="mode",
    )(parts, gram_frames, z)


def local(tensor, first_factor, second_factor):
    frame_count, col_count, row_count = tensor.shape
    components = first_factor.shape[0]
    row_size, col_size = lax.axis_size("row"), lax.axis_size("col")
    every = row_size * col_size
    share_rows = row_count // col_size
    direct = share_rows % 128 == 0
    shares = col_size if direct else 1

    def whole(stack):
        return stack if direct else jnp.moveaxis(stack, 0, 1).reshape(1, components, row_count)

    def cut(stack):
        return stack if direct else jnp.moveaxis(stack.reshape(components, col_size, share_rows), 1, 0)

    padded = jnp.pad(second_factor, ((0, 0), (0, -col_count % 128)))
    joined = jnp.concatenate([first_factor, padded], axis=1)
    joined = exchange(jnp.broadcast_to(joined, (col_size, *joined.shape)), "col")
    turned, wide = prepare(tensor, second_factor.astype(F32))
    first_full, grams, gram_second = assemble(
        whole(joined[:, :, :share_rows]), joined[:, :, share_rows:], row_size
    )
    grams = exchange(grams, "row")
    frame_part = project(first_full, second_factor.T.astype(F32), turned)
    inverse_first = inverse_of(grams, gram_second)
    frame_parts = exchange(frame_part.reshape(every, 1, -1), BOTH)
    frame_sum = exchange(spread_sum(frame_parts), BOTH).reshape(components, frame_count)
    frames, gram_frames, z, out = slab(inverse_first, frame_sum, wide, turned, shares)

    first_parts = exchange(cut(out), "col")
    inverse_second = inverse_of(gram_second[None], gram_frames)
    new_first = exchange(update(inverse_second, first_parts, col_size), "col")
    second_parts = exchange(second(whole(new_first), z, row_size), "row")
    final = exchange(cut(mode(second_parts, gram_frames, z, shares)), "col")
    return (frames, tree_sum([final[n] for n in range(col_size)]))


def solution(mesh):
    return jax.shard_map(
        local,
        mesh=mesh,
        in_specs=(P(None, "col", "row"), P(None, ("row", "col")), P(None, "col")),
        out_specs=(P(), P(None, ("row", "col"))),
        check_vma=False,
    )
```

time: 140 us -> 142 us (1.014)
  starting transfers between devices: 74 us -> 17.2 us
  blocking collectives: 0 us -> 42.5 us
  local copies, waits for them, and re-layouts: 5.37 us -> 29.9 us
  waiting for transfers between devices: 19.3 us -> 9.46 us
    ppermute x54 -> x0, starting transfers between devices: 74 us -> none  [swap(): return lax.ppermute(x, axes, [(n, n ^ offset) for n in range(count)])]
    all_to_all x0 -> x4, blocking collectives: none -> 42.5 us  [exchange(): return lax.all_to_all(x, axes, 0, 0)]
    unnamed x6 -> x17, local copies, waits for them, and re-layouts: 4.59 us -> 28.2 us
    ppermute x54 -> x0, waiting for transfers between devices: 19.3 us -> none  [swap(): return lax.ppermute(x, axes, [(n, n ^ offset) for n in range(count)])]
    all_to_all x0 -> x4, starting transfers between devices: none -> 17.2 us  [exchange(): return lax.all_to_all(x, axes, 0, 0)]
    all_to_all x0 -> x4, waiting for transfers between devices: none -> 9.46 us  [exchange(): return lax.all_to_all(x, axes, 0, 0)]
    pallas_call x9 -> x8, Pallas kernels: 28.2 us -> 29.6 us  [the longest x2 10.9 us: inverse_of(): pl.pallas_call(inverse_body, out_shape=jax.ShapeDtypeStruct(other.shape,...]
  transfers between devices with their start and end apart: 54 -> 4, of which waited for: 9 -> 3; matrix products, arithmetic and copies ran while one was open for 1% -> 1% of each run, Pallas kernels for 17% -> 12%
where the time goes in v1:
time: 142 us; the launch traced here: 141 us
  blocking collectives  42.5 us (30%)
  Pallas kernels  40.1 us (28%)
  local copies, waits for them, and re-layouts  29.9 us (21%)
  starting transfers between devices  17.2 us (12%)
  waiting for transfers between devices  9.46 us (7%)
    all_to_all x4, blocking collectives, exchange(): return lax.all_to_all(x, axes, 0, 0)  42.5 us
    unnamed x17, local copies, waits for them, and re-layouts  28.2 us
    all_to_all x4, starting transfers between devices, exchange(): return lax.all_to_all(x, axes, 0, 0)  17.2 us
    pallas_call x2, Pallas kernels, inverse_of(): pl.pallas_call(inverse_body, out_shape=jax.ShapeDtypeStruct(other.shape,...  10.9 us
    all_to_all x4, waiting for transfers between devices, exchange(): return lax.all_to_all(x, axes, 0, 0)  9.46 us
    pallas_call x1, Pallas kernels, slab(): pl.pallas_call(slab_body, out_shape=(jax.ShapeDtypeStruct((components, fr...  8.1 us
    pallas_call x1, Pallas kernels, mode(): pl.pallas_call(mode_body, out_shape=jax.ShapeDtypeStruct((shares, compone...  7.2 us
    pallas_call x1, Pallas kernels, prepare(): pl.pallas_call(functools.partial(prepare_body, groups), out_shape=(VM((co...  6.09 us
  transfers between devices with their start and end apart: 4, of which 3 were waited for; matrix products, arithmetic and copies ran while one was open for 1% of the time, Pallas kernels for 12%

profile of v1, /device:TPU:0, one launch (start us, length us, event | category | flops | bytes accessed | tf_op | source)
XLA Modules:
  0.0 141.3 jit_solution(11234769928276228830)
XLA Ops:
  3.0 7.3 %all-to-all-start = ((bf16[8,64,256]{2,1,0:T(8,128)(2,1)}), bf16[8,64,256]{2,1,0:T(8,128)(2,1)S(1)}, u32[]{:S(2)}, u32[]{:S(2)}) async-start(bf16[8,64,256]{2,1,0:T(8,128)(2,1)} %broadcast_in_dim.6), calls=%async_computation | async-start | bytes 524288 | tf_op jit(solution)/shard_map/all_to_all | solution.py:41
  11.1 4.6 %copy-done.6 = bf16[128,48,1024]{2,1,0:T(8,128)(2,1)S(1)} copy-done((bf16[128,48,1024]{2,1,0:T(8,128)(2,1)S(1)}, bf16[128,48,1024]{2,1,0:T(8,128)(2,1)}, u32[]{:S(2)}) %copy-start.6) | copy-done | bytes 12582936
  15.7 6.1 %prepare.1 = (bf16[48,128,1024]{2,1,0:T(8,128)(2,1)S(1)}, f32[48,64,128]{2,1,0:T(8,128)S(1)}) custom-call(bf16[128,48,1024]{2,1,0:T(8,128)(2,1)S(1)} %copy-done.6, f32[64,48]{1,0:T(8,128)S(1)} %copy.7.b_ref), custom_call_target="tpu_custom_call" | custom-call | tf_op jit(solution)/shard_map/prepare/pallas_call | solution.py:73
  21.8 4.5 %copy-done = bf16[48,128,1024]{2,1,0:T(8,128)(2,1)} copy-done((bf16[48,128,1024]{2,1,0:T(8,128)(2,1)}, bf16[48,128,1024]{2,1,0:T(8,128)(2,1)S(1)}, u32[]{:S(2)}) %copy-start) | copy-done | bytes 12582936
  27.3 4.6 %copy-done.1 = bf16[48,128,1024]{2,1,0:T(8,128)(2,1)S(1)} copy-done((bf16[48,128,1024]{2,1,0:T(8,128)(2,1)S(1)}, bf16[48,128,1024]{2,1,0:T(8,128)(2,1)}, u32[]{:S(2)}) %copy-start.1) | copy-done | bytes 12582936
  31.9 4.5 %project.1 = f32[64,128]{1,0:T(8,128)S(1)} custom-call(bf16[64,1024]{1,0:T(8,128)(2,1)S(1)} %get-tuple-element.13.full_ref, f32[48,64]{1,0:T(8,128)S(1)} %convert_bitcast_fusion.second_ref, bf16[48,128,1024]{2,1,0:T(8,128)(2,1)S(1)} %copy-done.1), custom_call_target="tpu_custom_call" | custom-call | tf_op jit(solution)/shard_map/project/pallas_call | solution.py:141
  36.4 13.0 %all_to_all.40.parts_ref = f32[32,1,256]{2,1,0:T(1,128)S(1)} all-to-all(f32[32,1,256]{2,1,0:T(1,128)S(1)} %bitcast.8), channel_id=1, replica_groups=mesh['row'=4,'col'=8] {'row','col'}, dimensions={0} | all-to-all | bytes 65536 | tf_op jit(solution)/shard_map/all_to_all | solution.py:41
  49.4 3.3 %all-to-all-start.1 = ((f32[4,64,128]{2,1,0:T(8,128)}), f32[4,64,128]{2,1,0:T(8,128)S(1)}, u32[]{:S(2)}, u32[]{:S(2)}) async-start(f32[4,64,128]{2,1,0:T(8,128)} %get-tuple-element.11), calls=%async_computation.1 | async-start | bytes 262144 | tf_op jit(solution)/shard_map/all_to_all | solution.py:41
  53.4 4.0 %all-to-all-done.1.grams_ref = f32[4,64,128]{2,1,0:T(8,128)S(1)} async-done(((f32[4,64,128]{2,1,0:T(8,128)}), f32[4,64,128]{2,1,0:T(8,128)S(1)}, u32[]{:S(2)}, u32[]{:S(2)}) %all-to-all-start.1) | async-done | bytes 131104 | tf_op jit(solution)/shard_map/all_to_all | solution.py:41
  57.3 2.6 %all-to-all-start.3 = ((f32[32,1,256]{2,1,0:T(1,128)}), f32[32,1,256]{2,1,0:T(1,128)S(1)}, u32[]{:S(2)}, u32[]{:S(2)}) async-start(f32[32,1,256]{2,1,0:T(1,128)} %spread_sum.1), calls=%async_computation.3 | async-start | bytes 65536 | tf_op jit(solution)/shard_map/all_to_all | solution.py:41
  59.9 5.5 %inverse.2.inverse_ref = f32[64,64]{1,0:T(8,128)S(1)} custom-call(f32[4,64,128]{2,1,0:T(8,128)S(1)} %all-to-all-done.1.grams_ref, f32[64,64]{1,0:T(8,128)S(1)} %get-tuple-element.12.other_ref), custom_call_target="tpu_custom_call" | custom-call | tf_op jit(solution)/shard_map/inverse/pallas_call | solution.py:173
  65.4 1.7 %all-to-all-done.3 = f32[32,1,256]{2,1,0:T(1,128)S(1)} async-done(((f32[32,1,256]{2,1,0:T(1,128)}), f32[32,1,256]{2,1,0:T(1,128)S(1)}, u32[]{:S(2)}, u32[]{:S(2)}) %all-to-all-start.3) | async-done | bytes 32800 | tf_op jit(solution)/shard_map/all_to_all | solution.py:41
  67.1 4.6 %copy-done.2 = bf16[48,128,1024]{2,1,0:T(8,128)(2,1)S(1)} copy-done((bf16[48,128,1024]{2,1,0:T(8,128)(2,1)S(1)}, bf16[48,128,1024]{2,1,0:T(8,128)(2,1)}, u32[]{:S(2)}) %copy-start.2) | copy-done | bytes 12582936
  71.7 8.1 %slab.1 = (f32[64,128]{1,0:T(8,128)}, f32[64,64]{1,0:T(8,128)S(1)}, f32[48,64,1024]{2,1,0:T(8,128)S(1)}, f32[8,64,128]{2,1,0:T(8,128)}) custom-call(f32[64,64]{1,0:T(8,128)S(1)} %inverse.2.inverse_ref, f32[64,128]{1,0:T(8,128)S(1)} %bitcast.7, f32[48,64,128]{2,1,0:T(8,128)S(1)} %get-tuple-element.15.wide_ref, bf16[48,128,1024]{2,1,0:T(8,128)(2,1)S(1)} %copy-done.2), custom_call_target="tpu_custom_call" | custom-call | tf_op jit(solution)/shard_map/slab/pallas_call | solution.py:239
  79.8 4.5 %copy-done.3 = f32[48,64,1024]{2,1,0:T(8,128)} copy-done((f32[48,64,1024]{2,1,0:T(8,128)}, f32[48,64,1024]{2,1,0:T(8,128)S(1)}, u32[]{:S(2)}) %copy-start.3) | copy-done | bytes 12582936
  84.3 4.1 %all-to-all-start.4 = ((f32[8,64,128]{2,1,0:T(8,128)}), f32[8,64,128]{2,1,0:T(8,128)S(1)}, u32[]{:S(2)}, u32[]{:S(2)}) async-start(f32[8,64,128]{2,1,0:T(8,128)} %get-tuple-element.18), calls=%async_computation.4 | async-start | bytes 524288 | tf_op jit(solution)/shard_map/all_to_all | solution.py:41
  88.4 5.5 %inverse.3.inverse_ref = f32[64,64]{1,0:T(8,128)S(1)} custom-call(f32[1,64,64]{2,1,0:T(8,128)S(1)} %bitcast.9, f32[64,64]{1,0:T(8,128)S(1)} %get-tuple-element.17.other_ref.gram_frames_ref), custom_call_target="tpu_custom_call" | custom-call | tf_op jit(solution)/shard_map/inverse/pallas_call | solution.py:173
  93.9 3.8 %all-to-all-done.4.parts_ref = f32[8,64,128]{2,1,0:T(8,128)S(1)} async-done(((f32[8,64,128]{2,1,0:T(8,128)}), f32[8,64,128]{2,1,0:T(8,128)S(1)}, u32[]{:S(2)}, u32[]{:S(2)}) %all-to-all-start.4) | async-done | bytes 262176 | tf_op jit(solution)/shard_map/all_to_all | solution.py:41
  97.8 10.7 %all_to_all.41.pieces_ref = bf16[8,64,128]{2,1,0:T(8,128)(2,1)S(1)} all-to-all(bf16[8,64,128]{2,1,0:T(8,128)(2,1)S(1)} %update.1), channel_id=1, replica_groups=mesh['row'=4,'col'=8] {'col'}, dimensions={0} | all-to-all | bytes 262144 | tf_op jit(solution)/shard_map/all_to_all | solution.py:41
  108.6 4.6 %copy-done.4 = f32[48,64,1024]{2,1,0:T(8,128)S(1)} copy-done((f32[48,64,1024]{2,1,0:T(8,128)S(1)}, f32[48,64,1024]{2,1,0:T(8,128)}, u32[]{:S(2)}) %copy-start.4) | copy-done | bytes 12582936
  113.1 1.6 %second.1 = f32[4,64,128]{2,1,0:T(8,128)S(1)} custom-call(bf16[8,64,128]{2,1,0:T(8,128)(2,1)S(1)} %all_to_all.41.pieces_ref, f32[48,64,1024]{2,1,0:T(8,128)S(1)} %copy-done.4), custom_call_target="tpu_custom_call" | custom-call | tf_op jit(solution)/shard_map/second/pallas_call | solution.py:300
  114.8 7.5 %all_to_all.42.parts_ref = f32[4,64,128]{2,1,0:T(8,128)S(1)} all-to-all(f32[4,64,128]{2,1,0:T(8,128)S(1)} %second.1), channel_id=1, replica_groups=mesh['row'=4,'col'=8] {'row'}, dimensions={0} | all-to-all | bytes 262144 | tf_op jit(solution)/shard_map/all_to_all | solution.py:41
  122.2 7.2 %mode.1 = f32[8,64,128]{2,1,0:T(8,128)S(1)} custom-call(f32[4,64,128]{2,1,0:T(8,128)S(1)} %all_to_all.42.parts_ref, f32[64,64]{1,0:T(8,128)S(1)} %get-tuple-element.17.other_ref.gram_frames_ref, f32[48,64,1024]{2,1,0:T(8,128)S(1)} %copy-done.5), custom_call_target="tpu_custom_call" | custom-call | tf_op jit(solution)/shard_map/mode/pallas_call | solution.py:332
  129.4 11.2 %all_to_all.43 = f32[8,64,128]{2,1,0:T(8,128)S(1)} all-to-all(f32[8,64,128]{2,1,0:T(8,128)S(1)} %mode.1), channel_id=1, replica_groups=mesh['row'=4,'col'=8] {'col'}, dimensions={0} | all-to-all | bytes 524288 | tf_op jit(solution)/shard_map/all_to_all | solution.py:41
  (22 shorter events, 5.6 us)
Async XLA Ops:
  0.6 25.7 %copy-start.7 = (bf16[64,48]{0,1:T(8,128)(2,1)S(1)}, bf16[64,48]{0,1:T(8,128)(2,1)}, u32[]{:S(2)}) copy-start(bf16[64,48]{0,1:T(8,128)(2,1)} %param.5) | copy-start | bytes 18436
  3.0 23.3 %all-to-all-start = ((bf16[8,64,256]{2,1,0:T(8,128)(2,1)}), bf16[8,64,256]{2,1,0:T(8,128)(2,1)S(1)}, u32[]{:S(2)}, u32[]{:S(2)}) async-start(bf16[8,64,256]{2,1,0:T(8,128)(2,1)} %broadcast_in_dim.6), calls=%async_computation | async-start | bytes 524288 | tf_op jit(solution)/shard_map/all_to_all | solution.py:41
  11.1 4.6 %copy-start.6 = (bf16[128,48,1024]{2,1,0:T(8,128)(2,1)S(1)}, bf16[128,48,1024]{2,1,0:T(8,128)(2,1)}, u32[]{:S(2)}) copy-start(bf16[128,48,1024]{2,1,0:T(8,128)(2,1)} %t_ref.1) | copy-start | bytes 37748740
  21.8 4.5 %copy-start = (bf16[48,128,1024]{2,1,0:T(8,128)(2,1)}, bf16[48,128,1024]{2,1,0:T(8,128)(2,1)S(1)}, u32[]{:S(2)}) copy-start(bf16[48,128,1024]{2,1,0:T(8,128)(2,1)S(1)} %get-tuple-element.14.t_ref) | copy-start | bytes 37748740
  27.3 4.6 %copy-start.1 = (bf16[48,128,1024]{2,1,0:T(8,128)(2,1)S(1)}, bf16[48,128,1024]{2,1,0:T(8,128)(2,1)}, u32[]{:S(2)}) copy-start(bf16[48,128,1024]{2,1,0:T(8,128)(2,1)} %copy-done) | copy-start | bytes 37748740
  49.4 7.9 %all-to-all-start.1 = ((f32[4,64,128]{2,1,0:T(8,128)}), f32[4,64,128]{2,1,0:T(8,128)S(1)}, u32[]{:S(2)}, u32[]{:S(2)}) async-start(f32[4,64,128]{2,1,0:T(8,128)} %get-tuple-element.11), calls=%async_computation.1 | async-start | bytes 262144 | tf_op jit(solution)/shard_map/all_to_all | solution.py:41
  57.3 9.8 %all-to-all-start.3 = ((f32[32,1,256]{2,1,0:T(1,128)}), f32[32,1,256]{2,1,0:T(1,128)S(1)}, u32[]{:S(2)}, u32[]{:S(2)}) async-start(f32[32,1,256]{2,1,0:T(1,128)} %spread_sum.1), calls=%async_computation.3 | async-start | bytes 65536 | tf_op jit(solution)/shard_map/all_to_all | solution.py:41
  67.1 4.6 %copy-start.2 = (bf16[48,128,1024]{2,1,0:T(8,128)(2,1)S(1)}, bf16[48,128,1024]{2,1,0:T(8,128)(2,1)}, u32[]{:S(2)}) copy-start(bf16[48,128,1024]{2,1,0:T(8,128)(2,1)} %copy-done) | copy-start | bytes 37748740
  79.8 4.5 %copy-start.3 = (f32[48,64,1024]{2,1,0:T(8,128)}, f32[48,64,1024]{2,1,0:T(8,128)S(1)}, u32[]{:S(2)}) copy-start(f32[48,64,1024]{2,1,0:T(8,128)S(1)} %get-tuple-element.19.z_ref) | copy-start | bytes 37748740
  84.3 13.3 %all-to-all-start.4 = ((f32[8,64,128]{2,1,0:T(8,128)}), f32[8,64,128]{2,1,0:T(8,128)S(1)}, u32[]{:S(2)}, u32[]{:S(2)}) async-start(f32[8,64,128]{2,1,0:T(8,128)} %get-tuple-element.18), calls=%async_computation.4 | async-start | bytes 524288 | tf_op jit(solution)/shard_map/all_to_all | solution.py:41
  108.5 4.6 %copy-start.4 = (f32[48,64,1024]{2,1,0:T(8,128)S(1)}, f32[48,64,1024]{2,1,0:T(8,128)}, u32[]{:S(2)}) copy-start(f32[48,64,1024]{2,1,0:T(8,128)} %copy-done.3) | copy-start | bytes 37748740
  113.1 9.1 %copy-start.5 = (f32[48,64,1024]{2,1,0:T(8,128)S(1)}, f32[48,64,1024]{2,1,0:T(8,128)}, u32[]{:S(2)}) copy-start(f32[48,64,1024]{2,1,0:T(8,128)} %copy-done.3) | copy-start | bytes 37748740
